TPU v7x, 512 devices: a whole 4x4x16 slice. The times are simulated.
512 devices in a mesh: hist: 64 (over z_lo, x, y), dom: 8 (over z_hi, core).
Axes of the slice: x: 4, y: 4, z: 16 (z_hi: 4, z_lo: 4; z = z_hi * 4 + z_lo), core: 2. Of those that a mesh axis runs over, the one named last changes fastest.
Arguments:
- coords: float32 [6, 1048576], P(None, ('dom', 'hist')), may hold values from -3 to 3
- charge: float32 [1048576], P(('dom', 'hist')), may hold values from 0.02 to 0.2
- row_index: int32 [1048576], P(('dom', 'hist')), may hold values from 0 to 511, as said below
- block_col: int32 [8192], P(('dom', 'hist')), may hold values from 0 to 496
- col_offset: int32 [1048576], P(('dom', 'hist')), may hold values from 0 to 15
- transfer_map: float32 [6, 84], replicated
- history: bfloat16 [512, 2, 512, 512], P('hist', None, 'dom'), may hold values from -16 to 16
- retard_index: int32 [512], P('hist'), may hold values from 0 to 16
- retard_frac: float32 [512], P('hist'), may hold values from 0 to 1
- retard_weight: float32 [512], P('hist'), may hold values from 0.005 to 0.05
- z_kernel: float32 [512, 512], P(None, 'dom')
- x_kernel: float32 [512, 512], replicated
Outputs:
- kicked: float32 [6, 1048576], P(None, ('dom', 'hist'))
- field: float32 [2, 512, 512], P(None, 'dom', 'hist')
- deposit: float32 [2, 512, 512], P(None, 'dom', 'hist')
Inputs may be any that keep to these rules, and one draw needn't show every extreme that they name: `row_index`: particle i lies in grid slab i // (1048576 // 8): its row is that slab's number times 64 plus 0 to 63.
All inputs are finite; a program needn't handle non-finite values.
Results may differ from a plain program's by a relative error of at most 0.0019.
Values may be sent and summed in bfloat16 or wider, within the bound.
A program may use at most 64 MiB of HBM per device.

v0:
```python
import jax
import jax.numpy as jnp
from jax import lax
from jax.sharding import PartitionSpec as P


def monomials(coords):
    products = [jnp.ones_like(coords[0])]
    for first in range(6):
        products.append(coords[first])
    for first in range(6):
        for second in range(first, 6):
            products.append(coords[first] * coords[second])
    for first in range(6):
        for second in range(first, 6):
            for third in range(second, 6):
                products.append(coords[first] * coords[second] * coords[third])
    return jnp.stack(products)


def retarded_source(history, retard_index, retard_frac, retard_weight):
    count_steps, comps, rows_here, width = history.shape

    def add_step(position, total):
        frame = lax.dynamic_index_in_dim(history, position, 0, keepdims=False).astype(jnp.float32)
        padded = jnp.pad(frame, ((0, 0), (0, 0), (width + 1, 0)))
        lag = retard_index[position]
        near = lax.dynamic_slice_in_dim(padded, width + 1 - lag, width, 2)
        far = lax.dynamic_slice_in_dim(padded, width - lag, width, 2)
        fraction = retard_frac[position]
        return total + retard_weight[position] * ((1.0 - fraction) * near + fraction * far)

    start = jnp.zeros((comps, rows_here, width), jnp.float32)
    return lax.fori_loop(0, count_steps, add_step, start)


def local(
    coords,
    charge,
    row_index,
    block_col,
    col_offset,
    transfer_map,
    history,
    retard_index,
    retard_frac,
    retard_weight,
    z_kernel,
    x_kernel,
):
    highest = lax.Precision.HIGHEST
    slab_rows = history.shape[2]
    width = history.shape[3]
    strip_width = width // lax.axis_size("hist")
    particles = coords.shape[1]
    group_size = min(1024, particles)
    count_groups = particles // group_size
    block_size = particles // block_col.shape[0]
    slab_start = lax.axis_index("dom") * slab_rows
    source = retarded_source(history, retard_index, retard_frac, retard_weight)
    spread = jnp.einsum("crx,xy->cry", source, x_kernel, precision=highest)
    partial_field = jnp.einsum("rs,csy->cry", z_kernel, spread, precision=highest)
    total_field = lax.psum(partial_field, ("hist", "dom"))
    slab_field = lax.dynamic_slice_in_dim(total_field, slab_start, slab_rows, 1)
    field_out = lax.dynamic_slice_in_dim(
        slab_field, lax.axis_index("hist") * strip_width, strip_width, 2
    )
    slab_rounded = slab_field.astype(jnp.bfloat16)
    folded = jnp.transpose(slab_rounded, (1, 0, 2)).reshape(slab_rows, 2 * width)
    pushed = jnp.dot(transfer_map, monomials(coords), precision=highest)
    column = jnp.repeat(block_col, block_size) + col_offset
    local_row = row_index - slab_start
    weight_pair = jnp.stack([charge, charge * pushed[1]]).astype(jnp.bfloat16)
    row_groups = local_row.reshape(count_groups, group_size)
    column_groups = column.reshape(count_groups, group_size)
    weight_groups = jnp.transpose(weight_pair.reshape(2, count_groups, group_size), (1, 0, 2))
    row_iota = lax.iota(jnp.int32, slab_rows)
    column_iota = lax.iota(jnp.int32, width)

    def one_group(accumulated, pieces):
        group_rows, group_columns, group_weights = pieces
        row_hot = (row_iota[:, None] == group_rows[None, :]).astype(jnp.bfloat16)
        column_hot = (group_columns[:, None] == column_iota[None, :]).astype(jnp.bfloat16)
        weighted = jnp.concatenate(
            [group_weights[0][:, None] * column_hot, group_weights[1][:, None] * column_hot], axis=1
        )
        accumulated = accumulated + jnp.dot(row_hot, weighted, preferred_element_type=jnp.float32)
        sampled_rows = lax.dot_general(
            row_hot, folded, (((0,), (0,)), ((), ())), preferred_element_type=jnp.float32
        )
        column_mask = column_hot.astype(jnp.float32)
        longitudinal = jnp.sum(sampled_rows[:, :width] * column_mask, axis=1)
        transverse = jnp.sum(sampled_rows[:, width:] * column_mask, axis=1)
        return (accumulated, jnp.stack([longitudinal, transverse]))

    empty = jnp.zeros((slab_rows, 2 * width), jnp.float32)
    deposit_local, sampled_groups = lax.scan(
        one_group, empty, (row_groups, column_groups, weight_groups)
    )
    sampled = jnp.transpose(sampled_groups, (1, 0, 2)).reshape(2, particles)
    deposit_split = lax.psum_scatter(
        deposit_local.reshape(slab_rows, 2, width), "hist", scatter_dimension=2, tiled=True
    )
    deposit_out = jnp.transpose(deposit_split, (1, 0, 2))
    kicked = pushed.at[5].add(0.5 * sampled[0]).at[1].add(0.5 * sampled[1])
    return (kicked, field_out, deposit_out)


def solution(mesh):
    return jax.shard_map(
        local,
        mesh=mesh,
        in_specs=(
            P(None, ("dom", "hist")),
            P(("dom", "hist")),
            P(("dom", "hist")),
            P(("dom", "hist")),
            P(("dom", "hist")),
            P(),
            P("hist", None, "dom", None),
            P("hist"),
            P("hist"),
            P("hist"),
            P(None, "dom"),
            P(),
        ),
        out_specs=(P(None, ("dom", "hist")), P(None, "dom", "hist"), P(None, "dom", "hist")),
        check_vma=False,
    )
```

profile of v0, /device:TPU:128, one launch (start us, length us, event | category | flops | bytes accessed | tf_op | source)
XLA Modules:
  0.0 956.1 jit_solution(17558240199381335158)
XLA Ops:
  7.2 76.3 %while.31 = (s32[]{:T(128)}, f32[2,64,512]{2,1,0:T(8,128)S(1)}, f32[8]{0:T(128)}, f32[8]{0:T(128)}, bf16[8,2,64,512]{3,2,1,0:T(8,128)(2,1)}, /*index=5*/s32[8]{0...) while((s32[]{:T(128)}, f32[2,64,512]{2,1,0:T(8,128)S(1)}, ...), condition=%wide.region_1.2_spmd.clone, body=%wide.region_0.1_spmd.clone.sunk | while | flops 524428 | bytes 1966899 | solution.py:34
  7.3 1.3 dynamic_slice.109
  8.6 1.3 dynamic_slice.108
  10.5 1.2 dynamic_slice.107
  14.3 0.9 dynamic-slice_bitcast_fusion.2
  15.2 0.1 pad_convert_fusion.2
  15.4 1.5 select_add_fusion.2
  16.9 1.2 dynamic_slice.109
  18.1 1.3 dynamic_slice.108
  20.0 1.2 dynamic_slice.107
  23.8 0.9 dynamic-slice_bitcast_fusion.2
  24.8 0.1 pad_convert_fusion.2
  24.9 1.5 select_add_fusion.2
  26.4 1.2 dynamic_slice.109
  27.6 1.3 dynamic_slice.108
  29.5 1.2 dynamic_slice.107
  33.4 0.9 dynamic-slice_bitcast_fusion.2
  34.4 1.5 select_add_fusion.2
  35.9 1.2 dynamic_slice.109
  37.2 1.3 dynamic_slice.108
  39.1 1.2 dynamic_slice.107
  42.9 0.9 dynamic-slice_bitcast_fusion.2
  43.9 1.5 select_add_fusion.2
  45.4 1.2 dynamic_slice.109
  46.7 1.3 dynamic_slice.108
  48.6 1.2 dynamic_slice.107
  52.4 0.9 dynamic-slice_bitcast_fusion.2
  53.5 1.5 select_add_fusion.2
  55.0 1.2 dynamic_slice.109
  56.2 1.3 dynamic_slice.108
  58.1 1.2 dynamic_slice.107
  61.9 0.9 dynamic-slice_bitcast_fusion.2
  63.0 1.5 select_add_fusion.2
  64.5 1.2 dynamic_slice.109
  65.7 1.3 dynamic_slice.108
  67.6 1.2 dynamic_slice.107
  71.5 0.9 dynamic-slice_bitcast_fusion.2
  72.5 1.5 select_add_fusion.2
  74.0 1.2 dynamic_slice.109
  75.3 1.3 dynamic_slice.108
  77.2 1.2 dynamic_slice.107
  81.0 0.9 dynamic-slice_bitcast_fusion.2
  82.0 1.5 select_add_fusion.2
  83.5 0.7 fusion.21
  84.3 3.2 convolution_bitcast_fusion
  88.3 1.1 stack.15
  89.4 0.5 fusion.34
  90.0 472.6 %all-reduce.3.cloned.1.call-done = f32[2,512,512]{1,2,0:T(8,128)} async-done(((f32[2,512,512]{1,2,0:T(8,128)}), f32[2,512,512]{1,2,0:T(8,128)}) %all-reduce.3.cloned.1.call-update) | async-done | bytes 2097168 | tf_op jit(solution)/shard_map/psum | solution.py:63
  562.6 1.2 dynamic-slice_convert_fusion
  563.8 0.1 copy.18
  563.9 5.3 while.32
  564.0 0.4 fusion.49
  564.4 0.8 fusion.50
  565.2 0.7 fusion.51
  566.0 0.5 fusion.52
  566.6 0.4 fusion.49
  567.1 0.8 fusion.50
  567.9 0.7 fusion.51
  568.6 0.5 fusion.52
  569.3 1.0 copy.19
  570.3 0.2 scatter-add.6
  570.5 0.2 scatter-add.9
  570.8 1.5 constant_dynamic-slice_fusion.2
  572.2 377.0 %reduce-scatter.2.cloned.1.call-done = f32[64,2,8]{0,2,1:T(8,128)} async-done(((f32[64,2,512]{0,2,1:T(8,128)}), f32[64,2,8]{0,2,1:T(8,128)}) %reduce-scatter.2.cloned.1.call-update) | async-done | bytes 4112 | tf_op jit(solution)/shard_map/reduce_scatter | solution.py:101
  (58 shorter events, 1.7 us)
Async XLA Ops:
  7.2 76.4 %copy-start = (f32[512,512]{1,0:T(8,128)S(1)}, f32[512,512]{1,0:T(8,128)}, u32[]{:S(2)}) copy-start(f32[512,512]{1,0:T(8,128)} %param.31) | copy-start | bytes 3145732
  7.2 555.4 %all-reduce.3.cloned.1.call-start = ((), (), s32[]{:S(2)}) async-start(), calls=%async_computation.1 | async-start | bytes 4194304 | tf_op jit(solution)/shard_map/psum | solution.py:63
  7.2 77.0 %copy-start.2 = (f32[512,64]{0,1:T(8,128)S(1)}, f32[512,64]{0,1:T(8,128)}, u32[]{:S(2)}) copy-start(f32[512,64]{0,1:T(8,128)} %param.30) | copy-start | bytes 393220
  84.3 3.3 copy-start.1
  84.3 3.5 copy-start.5
  84.3 3.5 copy-start.8
  87.5 0.7 copy-start.6
  87.5 1.9 copy-start.7
  87.5 2.4 copy-start.4
  87.5 861.8 %reduce-scatter.2.cloned.1.call-start = ((), (), s32[]{:S(2)}) async-start(), calls=%async_computation.2 | async-start | bytes 532480 | tf_op jit(solution)/shard_map/reduce_scatter | solution.py:101
  570.7 378.5 %copy-start.3 = (f32[6,2048]{1,0:T(8,128)}, f32[6,2048]{1,0:T(8,128)S(1)}, u32[]{:S(2)}) copy-start(f32[6,2048]{1,0:T(8,128)S(1)} %scatter-add.9) | copy-start | bytes 147460
Sparse Core Ops, SparseCore 0:
  87.6 474.9 all-reduce.2
  570.4 378.7 reduce-scatter.1
where the time goes:
time: 957 us; the launch traced here: 956 us
  waiting for transfers between devices  850 us (89%)
  local copies, waits for them, and re-layouts  43 us (4%)
  loops' own time  26.3 us (3%)
  other arithmetic  15.2 us (2%)
  between operations  14.3 us (1%)
    psum x1, waiting for transfers between devices, local(): total_field = lax.psum(partial_field, ('hist', 'dom'))  473 us
    reduce_scatter x1, waiting for transfers between devices, local(): lax.psum_scatter(deposit_local.reshape(slab_rows, 2, width), 'hist', scat...  377 us
    another operation x1, loops' own time, retarded_source(): return lax.fori_loop(0, count_steps, add_step, start)  26.2 us
  transfers between devices with their start and end apart: 2, of which 2 were waited for; matrix products, arithmetic and copies ran while one was open for 0% of the time, Pallas kernels for 0%

commit v1 on v0

v1 whole, which is shorter than its diff:
```python
import jax
import jax.numpy as jnp
from jax import lax
from jax.experimental import pallas as pl
from jax.experimental.pallas import tpu as pltpu
from jax.sharding import PartitionSpec as P

MESH = pl.DeviceIdType.MESH
F32 = jnp.float32
BF16 = jnp.bfloat16


def split(value):
    high = value.astype(BF16)
    return high, (value - high.astype(F32)).astype(BF16)


def dot_nn(a, b):
    return lax.dot_general(a, b, (((1,), (0,)), ((), ())), preferred_element_type=F32)


def dot_nt(a, b):
    return lax.dot_general(a, b, (((1,), (1,)), ((), ())), preferred_element_type=F32)


def dot_tn(a, b):
    return lax.dot_general(a, b, (((0,), (0,)), ((), ())), preferred_element_type=F32)


def kernel(
    coords_ref, charge_ref, row_ref, block_ref, offset_ref, map_ref, history_hbm, lag_ref, frac_ref,
    weight_ref, z_hbm, x_hbm,
    kicked_ref, field_ref, deposit_ref,
    history, x_full, z_own, near, far, x_high, x_low, z_high, z_low,
    a_send, a_recv, d_send, d_recv, e_send, e_recv, core_send, core_recv, ring_send, ring_recv,
    slab_t, column_hot, row_hot, pushed,
    load_sem, a_ssem, a_rsem, d_ssem, d_rsem, e_ssem, e_rsem, c_ssem, c_rsem, r_ssem, r_rsem,
    g_ssem, g_rsem,
):
    hist = lax.axis_index("hist")
    dom = lax.axis_index("dom")
    z_low_at, plane = hist // 16, hist % 16
    z_high_at, core = dom // 2, dom % 2
    z_at = z_high_at * 4 + z_low_at

    plane_peers = [{"hist": z_low_at * 16 + lax.rem(plane + k, 16), "dom": dom} for k in range(1, 16)]
    ring_at = [lax.rem(z_at + k, 16) for k in range(1, 16)]
    ring_peers = [{"hist": (at % 4) * 16 + plane, "dom": (at // 4) * 2 + core} for at in ring_at]
    low_at = [lax.rem(z_low_at + k, 4) for k in range(1, 4)]
    low_peers = [{"hist": at * 16 + plane, "dom": dom} for at in low_at]
    sibling = {"hist": hist, "dom": z_high_at * 2 + (1 - core)}

    load_history = pltpu.make_async_copy(history_hbm, history, load_sem.at[0])
    load_x = pltpu.make_async_copy(x_hbm, x_full, load_sem.at[1])
    load_z = pltpu.make_async_copy(z_hbm, z_own, load_sem.at[2])
    load_history.start()
    load_x.start()
    load_z.start()

    barrier = pltpu.get_barrier_semaphore()
    for peer in plane_peers + ring_peers + [sibling]:
        pl.semaphore_signal(barrier, inc=1, device_id=peer, device_id_type=MESH)

    lane = lax.broadcasted_iota(jnp.int32, (32, 128), 1)
    load_history.wait()

    def source_rows(group, carry):
        comp = group // 2
        row = pl.multiple_of((group % 2) * 32, 32)
        row_out = pl.multiple_of(group * 32, 32)
        near_sum = [jnp.zeros((32, 128), F32) for _ in range(4)]
        far_sum = [jnp.zeros((32, 128), F32) for _ in range(4)]
        for t in range(8):
            lag = lag_ref[t]
            fraction = frac_ref[t]
            weight = weight_ref[t]
            near_weight = weight * (1.0 - fraction)
            far_weight = weight * fraction
            inside = lane >= lag
            before = jnp.zeros((32, 128), F32)
            for j in range(4):
                piece = history[t, comp, pl.ds(row, 32), 128 * j : 128 * (j + 1)].astype(F32)
                turned = pltpu.roll(piece, lag, 1)
                moved = jnp.where(inside, turned, before)
                before = turned
                near_sum[j] = near_sum[j] + near_weight * moved
                far_sum[j] = far_sum[j] + far_weight * moved
        before = jnp.zeros((32, 128), F32)
        for j in range(4):
            turned = pltpu.roll(far_sum[j], 1, 1)
            near[pl.ds(row_out, 32), 128 * j : 128 * (j + 1)] = near_sum[j] + jnp.where(
                lane >= 1, turned, before
            )
            before = turned
        return carry

    lax.fori_loop(0, 4, source_rows, 0)

    load_x.wait()
    x_high[...], x_low[...] = split(x_full[...])
    s_high, s_low = split(near[...])
    twice = dot_nn(jnp.concatenate([s_high, s_low], axis=0), x_high[...])
    spread = twice[:128] + twice[128:] + dot_nn(s_high, x_low[...])
    spread_t = spread.T.reshape(4, 16, 8, 128)
    for zc in range(4):
        a_send[:, zc] = spread_t[zc]

    pl.semaphore_wait(barrier, 31)

    a_copies = []
    for k in range(1, 16):
        to = lax.rem(plane + k, 16)
        copy = pltpu.make_async_remote_copy(
            src_ref=a_send.at[to], dst_ref=a_recv.at[k - 1], send_sem=a_ssem.at[k - 1],
            recv_sem=a_rsem.at[k - 1], device_id=plane_peers[k - 1], device_id_type=MESH,
        )
        copy.start()
        a_copies.append(copy)

    load_z.wait()
    empty = jnp.zeros((64, 64), F32)
    for to in range(8):
        block = z_own[64 * to : 64 * (to + 1), :]
        pair = jnp.concatenate(
            [jnp.concatenate([block, empty], axis=1), jnp.concatenate([empty, block], axis=1)], axis=0
        )
        z_high[128 * to : 128 * (to + 1), :], z_low[128 * to : 128 * (to + 1), :] = split(pair)

    for chunk in range(4):
        lanes = slice(512 * chunk, 512 * (chunk + 1))
        wide = [jnp.broadcast_to(coords_ref[i : i + 1, lanes], (6, 512)) for i in range(6)]
        total = jnp.broadcast_to(map_ref[:, 0:1], (6, 512))
        at = 1
        for i in range(6):
            total = total + map_ref[:, at : at + 1] * wide[i]
            at += 1
        for i in range(6):
            for j in range(i, 6):
                total = total + map_ref[:, at : at + 1] * (wide[i] * wide[j])
                at += 1
        for i in range(6):
            for j in range(i, 6):
                two = wide[i] * wide[j]
                for k in range(j, 6):
                    total = total + map_ref[:, at : at + 1] * (two * wide[k])
                    at += 1
        pushed[:, lanes] = total

    row = row_ref[...] - dom * 64
    first = jnp.concatenate([jnp.full((1, 128), block_ref[b], jnp.int32) for b in range(16)], axis=1)
    column = first + offset_ref[...]
    place = ((column >> 3) & 15) * 32 + (column >> 7) * 8 + (column & 7)
    charge = charge_ref[...]
    weights = [charge.astype(BF16).astype(F32), (charge * pushed[1:2, :]).astype(BF16).astype(F32)]
    row_iota = lax.broadcasted_iota(jnp.int32, (64, 2048), 0)
    here = row_iota == row
    for c in range(2):
        row_hot[64 * c : 64 * (c + 1), :] = jnp.where(here, weights[c], 0.0).astype(BF16)
    place_iota = lax.broadcasted_iota(jnp.int32, (64, 2048), 0)

    def deposit_rows(step, carry):
        at = pl.multiple_of(step * 64, 64)
        hot = jnp.where(place_iota == place - at, 1.0, 0.0).astype(BF16)
        column_hot[pl.ds(at, 64), :] = hot
        rows = dot_nt(hot, row_hot[...]).astype(BF16)
        d_send[2 * step] = rows[:32]
        d_send[2 * step + 1] = rows[32:]
        return carry

    lax.fori_loop(0, 8, deposit_rows, 0)

    d_copies = []
    for k in range(1, 16):
        to = lax.rem(plane + k, 16)
        copy = pltpu.make_async_remote_copy(
            src_ref=d_send.at[to], dst_ref=d_recv.at[k - 1], send_sem=d_ssem.at[k - 1],
            recv_sem=d_rsem.at[k - 1], device_id=plane_peers[k - 1], device_id_type=MESH,
        )
        copy.start()
        d_copies.append(copy)

    for copy in a_copies:
        copy.wait_recv()
    part = a_send[plane]
    for k in range(15):
        part = part + a_recv[k]
    p_high, p_low = split(part.reshape(32, 128))
    twice = dot_nt(jnp.concatenate([p_high, p_low], axis=0), z_high[...])
    terms = twice[:32] + twice[32:] + dot_nt(p_high, z_low[...])
    for to in range(8):
        core_send[to % 2, to // 2] = terms[:, 128 * to : 128 * (to + 1)]
    core_copy = pltpu.make_async_remote_copy(
        src_ref=core_send.at[1 - core], dst_ref=core_recv, send_sem=c_ssem, recv_sem=c_rsem,
        device_id=sibling, device_id_type=MESH,
    )
    core_copy.start()
    core_copy.wait_recv()
    ring_send[...] = (core_send[core] + core_recv[...]).astype(BF16)

    r_copies = []
    for k in range(1, 16):
        copy = pltpu.make_async_remote_copy(
            src_ref=ring_send.at[ring_at[k - 1] // 4], dst_ref=ring_recv.at[k - 1],
            send_sem=r_ssem.at[k - 1], recv_sem=r_rsem.at[k - 1], device_id=ring_peers[k - 1],
            device_id_type=MESH,
        )
        copy.start()
        r_copies.append(copy)

    for copy in d_copies:
        copy.wait_recv()
    part = d_send[plane].astype(F32)
    for k in range(15):
        part = part + d_recv[k].astype(F32)
    e_send[...] = part.reshape(4, 8, 128)
    e_copies = []
    for k in range(1, 4):
        copy = pltpu.make_async_remote_copy(
            src_ref=e_send.at[low_at[k - 1]], dst_ref=e_recv.at[k - 1], send_sem=e_ssem.at[k - 1],
            recv_sem=e_rsem.at[k - 1], device_id=low_peers[k - 1], device_id_type=MESH,
        )
        copy.start()
        e_copies.append(copy)

    for copy in r_copies:
        copy.wait_recv()
    total = core_send[core, z_high_at] + core_recv[z_high_at]
    for k in range(15):
        total = total + ring_recv[k].astype(F32)
    slab_t[plane] = total.astype(BF16)
    g_copies = []
    for k in range(1, 16):
        copy = pltpu.make_async_remote_copy(
            src_ref=slab_t.at[plane], dst_ref=slab_t.at[plane], send_sem=g_ssem.at[k - 1],
            recv_sem=g_rsem.at[k - 1], device_id=plane_peers[k - 1], device_id_type=MESH,
        )
        copy.start()
        g_copies.append(copy)

    own = jnp.where(z_low_at == 0, total[0:8], 0.0)
    for zc in range(1, 4):
        own = own + jnp.where(z_low_at == zc, total[8 * zc : 8 * (zc + 1)], 0.0)
    field_ref[...] = own.T.reshape(2, 64, 8)
    for copy in e_copies:
        copy.wait_recv()
    own = e_send[z_low_at] + e_recv[0] + e_recv[1] + e_recv[2]
    deposit_ref[...] = own.T.reshape(2, 64, 8)
    kicked_ref[...] = pushed[...]

    for copy in g_copies:
        copy.wait_recv()
    sampled = dot_tn(slab_t[...].reshape(512, 128), column_hot[...])
    longitudinal = jnp.sum(jnp.where(here, sampled[:64], 0.0), axis=0, keepdims=True)
    transverse = jnp.sum(jnp.where(here, sampled[64:], 0.0), axis=0, keepdims=True)
    kicked_ref[5:6, :] = pushed[5:6, :] + 0.5 * longitudinal
    kicked_ref[1:2, :] = pushed[1:2, :] + 0.5 * transverse

    for copy in a_copies + d_copies + e_copies + [core_copy] + r_copies + g_copies:
        copy.wait_send()


def local(
    coords, charge, row_index, block_col, col_offset, transfer_map, history, retard_index, retard_frac,
    retard_weight, z_kernel, x_kernel,
):
    vmem = pl.BlockSpec(memory_space=pltpu.VMEM)
    smem = pl.BlockSpec(memory_space=pltpu.SMEM)
    anywhere = pl.BlockSpec(memory_space=pl.ANY)
    sem = pltpu.SemaphoreType.DMA
    return pl.pallas_call(
        kernel,
        out_shape=(
            jax.ShapeDtypeStruct((6, 2048), F32),
            jax.ShapeDtypeStruct((2, 64, 8), F32),
            jax.ShapeDtypeStruct((2, 64, 8), F32),
        ),
        in_specs=[
            vmem, vmem, vmem, smem, vmem, vmem, anywhere, smem, smem, smem, anywhere, anywhere,
        ],
        out_specs=(vmem, vmem, vmem),
        scratch_shapes=[
            pltpu.VMEM((8, 2, 64, 512), BF16),
            pltpu.VMEM((512, 512), F32),
            pltpu.VMEM((512, 64), F32),
            pltpu.VMEM((128, 512), F32),
            pltpu.VMEM((8, 128), F32),
            pltpu.VMEM((512, 512), BF16),
            pltpu.VMEM((512, 512), BF16),
            pltpu.VMEM((1024, 128), BF16),
            pltpu.VMEM((1024, 128), BF16),
            pltpu.VMEM((16, 4, 8, 128), F32),
            pltpu.VMEM((15, 4, 8, 128), F32),
            pltpu.VMEM((16, 32, 128), BF16),
            pltpu.VMEM((15, 32, 128), BF16),
            pltpu.VMEM((4, 8, 128), F32),
            pltpu.VMEM((3, 8, 128), F32),
            pltpu.VMEM((2, 4, 32, 128), F32),
            pltpu.VMEM((4, 32, 128), F32),
            pltpu.VMEM((4, 32, 128), BF16),
            pltpu.VMEM((15, 32, 128), BF16),
            pltpu.VMEM((16, 32, 128), BF16),
            pltpu.VMEM((512, 2048), BF16),
            pltpu.VMEM((128, 2048), BF16),
            pltpu.VMEM((6, 2048), F32),
            sem((3,)),
            sem((15,)), sem((15,)),
            sem((15,)), sem((15,)),
            sem((3,)), sem((3,)),
            sem, sem,
            sem((15,)), sem((15,)),
            sem((15,)), sem((15,)),
        ],
        compiler_params=pltpu.CompilerParams(
            collective_id=0, has_side_effects=True, vmem_limit_bytes=40 * 1024 * 1024
        ),
        cost_estimate=pl.CostEstimate(flops=10**9, bytes_accessed=4 * 10**6, transcendentals=0),
    )(
        coords,
        charge.reshape(1, -1),
        row_index.reshape(1, -1),
        block_col,
        col_offset.reshape(1, -1),
        transfer_map,
        history,
        retard_index,
        retard_frac,
        retard_weight,
        z_kernel,
        x_kernel,
    )


def solution(mesh):
    return jax.shard_map(
        local,
        mesh=mesh,
        in_specs=(
            P(None, ("dom", "hist")),
            P(("dom", "hist")),
            P(("dom", "hist")),
            P(("dom", "hist")),
            P(("dom", "hist")),
            P(),
            P("hist", None, "dom", None),
            P("hist"),
            P("hist"),
            P("hist"),
            P(None, "dom"),
            P(),
        ),
        out_specs=(P(None, ("dom", "hist")), P(None, "dom", "hist"), P(None, "dom", "hist")),
        check_vma=False,
    )
```

time: 957 us -> 45.9 us (0.05)
  the two profiles are of different devices: /device:TPU:128 before, /device:TPU:1 now
where the time goes in v1:
time: 45.9 us; the launch traced here: 45.7 us
  Pallas kernels  39.4 us (86%)
  local copies, waits for them, and re-layouts  5.54 us (12%)
  between operations  0.8 us (2%)
    pallas_call x1, Pallas kernels, local(): pl.pallas_call(kernel, out_shape=(jax.ShapeDtypeStruct((6, 2048), F32), j...  39.4 us
    unnamed x24, local copies, waits for them, and re-layouts  4.2 us
    pallas_call x2, local copies, waits for them, and re-layouts, local(): pl.pallas_call(kernel, out_shape=(jax.ShapeDtypeStruct((6, 2048), F32), j...  1.33 us

profile of v1, /device:TPU:1, one launch (start us, length us, event | category | flops | bytes accessed | tf_op | source)
XLA Modules:
  0.0 45.7 jit_solution(13244774368265435363)
XLA Ops:
  0.6 0.0 copy-start.2
  0.6 0.0 copy-start.3
  0.7 0.0 copy-start.4
  0.7 0.0 copy-start.5
  0.7 0.0 copy-start.6
  0.7 0.0 copy-start.7
  0.7 0.0 copy-start.8
  0.7 0.0 copy-start.9
  0.7 0.0 copy-start.10
  0.7 1.1 %copy.15.z_hbm = f32[512,64]{1,0:T(8,128)S(1)} copy(f32[512,64]{0,1:T(8,128)} %param.22) | data formatting | bytes 262144 | tf_op args[10]
  1.8 0.0 copy-done.2
  1.8 0.0 copy-done.3
  1.8 0.0 copy-done.4
  1.9 0.0 copy-done.5
  1.9 0.0 copy-done.6
  1.9 0.0 copy-done.7
  1.9 0.0 copy-done.8
  1.9 0.0 copy-done.9
  1.9 0.0 copy-done.10
  1.9 0.0 copy-start
  1.9 1.2 %copy-done = bf16[8,2,64,512]{3,2,1,0:T(8,128)(2,1)S(1)} copy-done((bf16[8,2,64,512]{3,2,1,0:T(8,128)(2,1)S(1)}, bf16[8,2,64,512]{3,2,1,0:T(8,128)(2,1)}, u32[]{:S(2)}) %copy-start) | copy-done | bytes 1048600
  3.1 0.0 copy-start.1
  3.1 1.2 %copy-done.1 = f32[512,512]{1,0:T(8,128)S(1)} copy-done((f32[512,512]{1,0:T(8,128)S(1)}, f32[512,512]{1,0:T(8,128)}, u32[]{:S(2)}) %copy-start.1) | copy-done | bytes 1048600
  4.4 39.4 %shard_map.139 = (f32[6,2048]{1,0:T(8,128)S(1)}, f32[2,64,8]{2,1,0:T(8,128)S(1)}, f32[2,64,8]{2,1,0:T(8,128)S(1)}) custom-call(f32[6,2048]{1,0:T(8,128)S(1)} %copy-done.2, f32[1,2048]{1,0:T(1,128)S(1)} %bitcast.3, s32[1,2048]{1,0:T(1,128)S(1)} %bitcast.4, s32[16]{0:T(128)S(1)} %copy-done.7, s32[1,2048]{1,0:T(1,128)S(1)} %bitcast.5, f32[6,84]{1,0:T(8,128)S(1)} %copy-done.6, ...), custom_call_target="tpu_custom_call" | custom-call | flops 1000000000 | bytes 4000000 | tf_op jit(solution)/shard_map/pallas_call | solution.py:270
  43.8 0.7 %copy.16 = f32[2,64,8]{1,2,0:T(8,128)} copy(f32[2,64,8]{2,1,0:T(8,128)S(1)} %get-tuple-element.4) | data formatting | bytes 8192 | tf_op jit(solution)/shard_map/pallas_call | solution.py:270
  44.4 0.7 %copy.17 = f32[2,64,8]{1,2,0:T(8,128)} copy(f32[2,64,8]{2,1,0:T(8,128)S(1)} %get-tuple-element.5) | data formatting | bytes 8192 | tf_op jit(solution)/shard_map/pallas_call | solution.py:270
  45.1 0.6 %copy.19 = f32[6,2048]{1,0:T(8,128)} copy(f32[6,2048]{1,0:T(8,128)S(1)} %get-tuple-element.9) | data formatting | bytes 98304
Async XLA Ops:
  0.6 1.2 %copy-start.2 = (f32[6,2048]{1,0:T(8,128)S(1)}, f32[6,2048]{1,0:T(8,128)}, u32[]{:S(2)}) copy-start(f32[6,2048]{1,0:T(8,128)} %coords_ref.1) | copy-start | bytes 147460
  0.6 1.2 %copy-start.3 = (f32[2048]{0:T(1024)S(1)}, f32[2048]{0:T(1024)}, u32[]{:S(2)}) copy-start(f32[2048]{0:T(1024)} %param.13) | copy-start | bytes 24580
  0.7 1.2 %copy-start.4 = (s32[2048]{0:T(1024)S(1)}, s32[2048]{0:T(1024)}, u32[]{:S(2)}) copy-start(s32[2048]{0:T(1024)} %param.14) | copy-start | bytes 24580
  0.7 1.2 %copy-start.5 = (s32[2048]{0:T(1024)S(1)}, s32[2048]{0:T(1024)}, u32[]{:S(2)}) copy-start(s32[2048]{0:T(1024)} %param.16) | copy-start | bytes 24580
  0.7 1.2 %copy-start.6 = (f32[6,84]{1,0:T(8,128)S(1)}, f32[6,84]{1,0:T(8,128)}, u32[]{:S(2)}) copy-start(f32[6,84]{1,0:T(8,128)} %map_ref.1) | copy-start | bytes 6052
  0.7 1.2 %copy-start.7 = (s32[16]{0:T(128)S(1)}, s32[16]{0:T(128)}, u32[]{:S(2)}) copy-start(s32[16]{0:T(128)} %block_ref.1) | copy-start | bytes 196
  0.7 1.2 %copy-start.8 = (s32[8]{0:T(128)S(1)}, s32[8]{0:T(128)}, u32[]{:S(2)}) copy-start(s32[8]{0:T(128)} %lag_ref.1) | copy-start | bytes 100
  0.7 1.2 %copy-start.9 = (f32[8]{0:T(128)S(1)}, f32[8]{0:T(128)}, u32[]{:S(2)}) copy-start(f32[8]{0:T(128)} %frac_ref.1) | copy-start | bytes 100
  0.7 1.2 %copy-start.10 = (f32[8]{0:T(128)S(1)}, f32[8]{0:T(128)}, u32[]{:S(2)}) copy-start(f32[8]{0:T(128)} %weight_ref.1) | copy-start | bytes 100
  1.9 1.2 %copy-start = (bf16[8,2,64,512]{3,2,1,0:T(8,128)(2,1)S(1)}, bf16[8,2,64,512]{3,2,1,0:T(8,128)(2,1)}, u32[]{:S(2)}) copy-start(bf16[8,2,64,512]{3,2,1,0:T(8,128)(2,1)} %history_hbm.1) | copy-start | bytes 3145732
  3.1 1.2 %copy-start.1 = (f32[512,512]{1,0:T(8,128)S(1)}, f32[512,512]{1,0:T(8,128)}, u32[]{:S(2)}) copy-start(f32[512,512]{1,0:T(8,128)} %x_hbm.1) | copy-start | bytes 3145732

commit v2 on v1

--- a/solution.py
+++ b/solution.py
@@ -28,14 +28,15 @@
 
 
 def kernel(
-    coords_ref, charge_ref, row_ref, block_ref, offset_ref, map_ref, history_hbm, lag_ref, frac_ref,
-    weight_ref, z_hbm, x_hbm,
+    coords_hbm, charge_hbm, row_hbm, block_hbm, offset_hbm, map_hbm, history_hbm, lag_hbm, frac_hbm,
+    weight_hbm, z_hbm, x_hbm,
     kicked_ref, field_ref, deposit_ref,
-    history, x_full, z_own, near, far, x_high, x_low, z_high, z_low,
+    coords_ref, charge_ref, row_ref, block_ref, offset_ref, map_ref, lag_ref, frac_ref, weight_ref,
+    history, x_full, z_own, near, x_high, x_low, z_high, z_low,
     a_send, a_recv, d_send, d_recv, e_send, e_recv, core_send, core_recv, ring_send, ring_recv,
     slab_t, column_hot, row_hot, pushed,
     load_sem, a_ssem, a_rsem, d_ssem, d_rsem, e_ssem, e_rsem, c_ssem, c_rsem, r_ssem, r_rsem,
-    g_ssem, g_rsem,
+    g_ssem, g_rsem, far_sem,
 ):
     hist = lax.axis_index("hist")
     dom = lax.axis_index("dom")
@@ -43,25 +44,42 @@
     z_high_at, core = dom // 2, dom % 2
     z_at = z_high_at * 4 + z_low_at
 
-    plane_peers = [{"hist": z_low_at * 16 + lax.rem(plane + k, 16), "dom": dom} for k in range(1, 16)]
-    ring_at = [lax.rem(z_at + k, 16) for k in range(1, 16)]
+    plane_steps = sorted(
+        [(a, b) for a in range(4) for b in range(4) if a or b],
+        key=lambda step: -(min(step[0], 4 - step[0]) + min(step[1], 4 - step[1])),
+    )
+    plane_at = [lax.rem(plane // 4 + a, 4) * 4 + lax.rem(plane % 4 + b, 4) for a, b in plane_steps]
+    plane_peers = [{"hist": z_low_at * 16 + at, "dom": dom} for at in plane_at]
+    ring_steps = sorted(range(1, 16), key=lambda k: -min(k, 16 - k))
+    ring_at = [lax.rem(z_at + k, 16) for k in ring_steps]
     ring_peers = [{"hist": (at % 4) * 16 + plane, "dom": (at // 4) * 2 + core} for at in ring_at]
+    ring_near = [peer for k, peer in zip(ring_steps, ring_peers) if min(k, 16 - k) <= 4]
+    ring_four = [peer for k, peer in zip(ring_steps, ring_peers) if min(k, 16 - k) == 4]
     low_at = [lax.rem(z_low_at + k, 4) for k in range(1, 4)]
     low_peers = [{"hist": at * 16 + plane, "dom": dom} for at in low_at]
     sibling = {"hist": hist, "dom": z_high_at * 2 + (1 - core)}
 
-    load_history = pltpu.make_async_copy(history_hbm, history, load_sem.at[0])
-    load_x = pltpu.make_async_copy(x_hbm, x_full, load_sem.at[1])
-    load_z = pltpu.make_async_copy(z_hbm, z_own, load_sem.at[2])
-    load_history.start()
-    load_x.start()
-    load_z.start()
-
+    def load(index, source, target):
+        copy = pltpu.make_async_copy(source, target, load_sem.at[index])
+        copy.start()
+        return copy
+
+    load_history = load(0, history_hbm, history)
+    load_steps = [load(1, lag_hbm, lag_ref), load(2, frac_hbm, frac_ref), load(3, weight_hbm, weight_ref)]
+    load_x = load(4, x_hbm, x_full)
     barrier = pltpu.get_barrier_semaphore()
-    for peer in plane_peers + ring_peers + [sibling]:
+    for peer in plane_peers + ring_near + [sibling]:
         pl.semaphore_signal(barrier, inc=1, device_id=peer, device_id_type=MESH)
 
+    load_z = load(5, z_hbm, z_own)
+    load_particles = [
+        load(6, coords_hbm, coords_ref), load(7, charge_hbm, charge_ref), load(8, row_hbm, row_ref),
+        load(9, block_hbm, block_ref), load(10, offset_hbm, offset_ref), load(11, map_hbm, map_ref),
+    ]
+
     lane = lax.broadcasted_iota(jnp.int32, (32, 128), 1)
+    for copy in load_steps:
+        copy.wait()
     load_history.wait()
 
     def source_rows(group, carry):
@@ -105,11 +123,13 @@
     for zc in range(4):
         a_send[:, zc] = spread_t[zc]
 
-    pl.semaphore_wait(barrier, 31)
+    pl.semaphore_wait(barrier, 24)
+    for peer in ring_four:
+        pl.semaphore_signal(far_sem, inc=1, device_id=peer, device_id_type=MESH)
 
     a_copies = []
     for k in range(1, 16):
-        to = lax.rem(plane + k, 16)
+        to = plane_at[k - 1]
         copy = pltpu.make_async_remote_copy(
             src_ref=a_send.at[to], dst_ref=a_recv.at[k - 1], send_sem=a_ssem.at[k - 1],
             recv_sem=a_rsem.at[k - 1], device_id=plane_peers[k - 1], device_id_type=MESH,
@@ -120,12 +140,14 @@
     load_z.wait()
     empty = jnp.zeros((64, 64), F32)
     for to in range(8):
-        block = z_own[64 * to : 64 * (to + 1), :]
+        block = z_own[:, 64 * to : 64 * (to + 1)]
         pair = jnp.concatenate(
             [jnp.concatenate([block, empty], axis=1), jnp.concatenate([empty, block], axis=1)], axis=0
         )
-        z_high[128 * to : 128 * (to + 1), :], z_low[128 * to : 128 * (to + 1), :] = split(pair)
-
+        z_high[:, 128 * to : 128 * (to + 1)], z_low[:, 128 * to : 128 * (to + 1)] = split(pair)
+
+    for copy in load_particles:
+        copy.wait()
     for chunk in range(4):
         lanes = slice(512 * chunk, 512 * (chunk + 1))
         wide = [jnp.broadcast_to(coords_ref[i : i + 1, lanes], (6, 512)) for i in range(6)]
@@ -171,7 +193,7 @@
 
     d_copies = []
     for k in range(1, 16):
-        to = lax.rem(plane + k, 16)
+        to = plane_at[k - 1]
         copy = pltpu.make_async_remote_copy(
             src_ref=d_send.at[to], dst_ref=d_recv.at[k - 1], send_sem=d_ssem.at[k - 1],
             recv_sem=d_rsem.at[k - 1], device_id=plane_peers[k - 1], device_id_type=MESH,
@@ -185,8 +207,8 @@
     for k in range(15):
         part = part + a_recv[k]
     p_high, p_low = split(part.reshape(32, 128))
-    twice = dot_nt(jnp.concatenate([p_high, p_low], axis=0), z_high[...])
-    terms = twice[:32] + twice[32:] + dot_nt(p_high, z_low[...])
+    twice = dot_nn(jnp.concatenate([p_high, p_low], axis=0), z_high[...])
+    terms = twice[:32] + twice[32:] + dot_nn(p_high, z_low[...])
     for to in range(8):
         core_send[to % 2, to // 2] = terms[:, 128 * to : 128 * (to + 1)]
     core_copy = pltpu.make_async_remote_copy(
@@ -197,6 +219,7 @@
     core_copy.wait_recv()
     ring_send[...] = (core_send[core] + core_recv[...]).astype(BF16)
 
+    pl.semaphore_wait(far_sem, 2)
     r_copies = []
     for k in range(1, 16):
         copy = pltpu.make_async_remote_copy(
@@ -240,11 +263,13 @@
     own = jnp.where(z_low_at == 0, total[0:8], 0.0)
     for zc in range(1, 4):
         own = own + jnp.where(z_low_at == zc, total[8 * zc : 8 * (zc + 1)], 0.0)
-    field_ref[...] = own.T.reshape(2, 64, 8)
+    field_ref[0] = own[:, :64]
+    field_ref[1] = own[:, 64:]
     for copy in e_copies:
         copy.wait_recv()
     own = e_send[z_low_at] + e_recv[0] + e_recv[1] + e_recv[2]
-    deposit_ref[...] = own.T.reshape(2, 64, 8)
+    deposit_ref[0] = own[:, :64]
+    deposit_ref[1] = own[:, 64:]
     kicked_ref[...] = pushed[...]
 
     for copy in g_copies:
@@ -259,35 +284,53 @@
         copy.wait_send()
 
 
+def place(kicked_in, field_in, deposit_in, kicked_ref, field_ref, deposit_ref, sems):
+    copies = [
+        pltpu.make_async_copy(kicked_in, kicked_ref, sems.at[0]),
+        pltpu.make_async_copy(field_in, field_ref, sems.at[1]),
+        pltpu.make_async_copy(deposit_in, deposit_ref, sems.at[2]),
+    ]
+    for copy in copies:
+        copy.start()
+    for copy in copies:
+        copy.wait()
+
+
 def local(
     coords, charge, row_index, block_col, col_offset, transfer_map, history, retard_index, retard_frac,
     retard_weight, z_kernel, x_kernel,
 ):
     vmem = pl.BlockSpec(memory_space=pltpu.VMEM)
-    smem = pl.BlockSpec(memory_space=pltpu.SMEM)
-    anywhere = pl.BlockSpec(memory_space=pl.ANY)
+    hbm = pl.BlockSpec(memory_space=pltpu.HBM)
     sem = pltpu.SemaphoreType.DMA
-    return pl.pallas_call(
+    shapes = (
+        jax.ShapeDtypeStruct((6, 2048), F32),
+        jax.ShapeDtypeStruct((2, 8, 64), F32),
+        jax.ShapeDtypeStruct((2, 8, 64), F32),
+    )
+    results = pl.pallas_call(
         kernel,
-        out_shape=(
-            jax.ShapeDtypeStruct((6, 2048), F32),
-            jax.ShapeDtypeStruct((2, 64, 8), F32),
-            jax.ShapeDtypeStruct((2, 64, 8), F32),
-        ),
-        in_specs=[
-            vmem, vmem, vmem, smem, vmem, vmem, anywhere, smem, smem, smem, anywhere, anywhere,
-        ],
+        out_shape=tuple(pltpu.VMEM(shape.shape, shape.dtype) for shape in shapes),
+        in_specs=[hbm] * 12,
         out_specs=(vmem, vmem, vmem),
         scratch_shapes=[
+            pltpu.VMEM((6, 2048), F32),
+            pltpu.VMEM((1, 2048), F32),
+            pltpu.VMEM((1, 2048), jnp.int32),
+            pltpu.SMEM((16,), jnp.int32),
+            pltpu.VMEM((1, 2048), jnp.int32),
+            pltpu.VMEM((6, 84), F32),
+            pltpu.SMEM((8,), jnp.int32),
+            pltpu.SMEM((8,), F32),
+            pltpu.SMEM((8,), F32),
             pltpu.VMEM((8, 2, 64, 512), BF16),
             pltpu.VMEM((512, 512), F32),
-            pltpu.VMEM((512, 64), F32),
+            pltpu.VMEM((64, 512), F32),
             pltpu.VMEM((128, 512), F32),
-            pltpu.VMEM((8, 128), F32),
             pltpu.VMEM((512, 512), BF16),
             pltpu.VMEM((512, 512), BF16),
-            pltpu.VMEM((1024, 128), BF16),
-            pltpu.VMEM((1024, 128), BF16),
+            pltpu.VMEM((128, 1024), BF16),
+            pltpu.VMEM((128, 1024), BF16),
             pltpu.VMEM((16, 4, 8, 128), F32),
             pltpu.VMEM((15, 4, 8, 128), F32),
             pltpu.VMEM((16, 32, 128), BF16),
@@ -302,16 +345,16 @@
             pltpu.VMEM((512, 2048), BF16),
             pltpu.VMEM((128, 2048), BF16),
             pltpu.VMEM((6, 2048), F32),
-            sem((3,)),
+            sem((12,)),
             sem((15,)), sem((15,)),
             sem((15,)), sem((15,)),
             sem((3,)), sem((3,)),
             sem, sem,
             sem((15,)), sem((15,)),
-            sem((15,)), sem((15,)),
+            sem((15,)), sem((15,)), pltpu.SemaphoreType.REGULAR,
         ],
         compiler_params=pltpu.CompilerParams(
-            collective_id=0, has_side_effects=True, vmem_limit_bytes=40 * 1024 * 1024
+            collective_id=0, has_side_effects=True, vmem_limit_bytes=58 * 1024 * 1024
         ),
         cost_estimate=pl.CostEstimate(flops=10**9, bytes_accessed=4 * 10**6, transcendentals=0),
     )(
@@ -325,9 +368,19 @@
         retard_index,
         retard_frac,
         retard_weight,
-        z_kernel,
+        z_kernel.T,
         x_kernel,
     )
+    anywhere = pl.BlockSpec(memory_space=pl.ANY)
+    kicked, field, deposit = pl.pallas_call(
+        place,
+        out_shape=shapes,
+        in_specs=[vmem] * 3,
+        out_specs=(anywhere,) * 3,
+        scratch_shapes=[sem((3,))],
+        cost_estimate=pl.CostEstimate(flops=0, bytes_accessed=10**5, transcendentals=0),
+    )(*[pltpu.with_memory_space_constraint(r, pltpu.VMEM) for r in results])
+    return kicked, jnp.swapaxes(field, 1, 2), jnp.swapaxes(deposit, 1, 2)
 
 
 def solution(mesh):

time: 45.9 us -> 38.6 us (0.84)
  local copies, waits for them, and re-layouts: 5.54 us -> 0 us
  Pallas kernels: 39.4 us -> 37.8 us
    unnamed x24 -> x0, local copies, waits for them, and re-layouts: 4.2 us -> none
    pallas_call x1 -> x2, Pallas kernels: 39.4 us -> 37.8 us  [the longest x1 37.2 us: local(): pl.pallas_call(kernel, out_shape=tuple((pltpu.VMEM(shape.shape, shape.dty...]
    pallas_call x2 -> x0, local copies, waits for them, and re-layouts: 1.33 us -> none  [local(): pl.pallas_call(kernel, out_shape=(jax.ShapeDtypeStruct((6, 2048), F32), j...]
where the time goes in v2:
time: 38.6 us; the launch traced here: 38.5 us
  Pallas kernels  37.8 us (98%)
  between operations  0.64 us (2%)
    pallas_call x1, Pallas kernels, local(): pl.pallas_call(kernel, out_shape=tuple((pltpu.VMEM(shape.shape, shape.dty...  37.2 us

profile of v2, /device:TPU:1, one launch (start us, length us, event | category | flops | bytes accessed | tf_op | source)
XLA Modules:
  0.0 38.5 jit_solution(18093351199581525721)
XLA Ops:
  0.6 37.2 %shard_map.139 = (f32[6,2048]{1,0:T(8,128)S(1)}, f32[2,8,64]{2,1,0:T(8,128)S(1)}, f32[2,8,64]{2,1,0:T(8,128)S(1)}) custom-call(f32[6,2048]{1,0:T(8,128)} %coords_hbm.1, f32[1,2048]{1,0:T(1,128)} %bitcast.7, s32[1,2048]{1,0:T(1,128)} %bitcast.8, s32[16]{0:T(128)} %block_hbm.1, s32[1,2048]{1,0:T(1,128)} %bitcast.9, f32[6,84]{1,0:T(8,128)} %map_hbm.1, ...), custom_call_target="tpu_custom_call" | custom-call | flops 1000000000 | bytes 4000000 | tf_op jit(solution)/shard_map/pallas_call | solution.py:311
  37.8 0.7 %shard_map.140 = (f32[6,2048]{1,0:T(8,128)}, f32[2,8,64]{2,1,0:T(8,128)}, f32[2,8,64]{2,1,0:T(8,128)}) custom-call(f32[6,2048]{1,0:T(8,128)S(1)} %get-tuple-element.9.kicked_in, f32[2,8,64]{2,1,0:T(8,128)S(1)} %get-tuple-element.10.field_in, f32[2,8,64]{2,1,0:T(8,128)S(1)} %get-tuple-element.11.deposit_in), custom_call_target="tpu_custom_call" | custom-call | bytes 100000 | tf_op jit(solution)/shard_map/pallas_call | solution.py:375

commit v3 on v2

--- a/solution.py
+++ b/solution.py
@@ -57,6 +57,17 @@
     ring_four = [peer for k, peer in zip(ring_steps, ring_peers) if min(k, 16 - k) == 4]
     low_at = [lax.rem(z_low_at + k, 4) for k in range(1, 4)]
     low_peers = [{"hist": at * 16 + plane, "dom": dom} for at in low_at]
+    def stage(buffer, send_sem, recv_sem):
+        return pltpu.make_async_remote_copy(
+            src_ref=buffer, dst_ref=buffer, send_sem=send_sem, recv_sem=recv_sem,
+            device_id=plane_peers[0], device_id_type=MESH,
+        )
+
+    a_stage = stage(a_recv, a_ssem, a_rsem)
+    d_stage = stage(d_recv, d_ssem, d_rsem)
+    e_stage = stage(e_recv, e_ssem, e_rsem)
+    r_stage = stage(ring_recv, r_ssem, r_rsem)
+    g_stage = stage(slab_t.at[0:15], g_ssem, g_rsem)
     sibling = {"hist": hist, "dom": z_high_at * 2 + (1 - core)}
 
     def load(index, source, target):
@@ -127,15 +138,13 @@
     for peer in ring_four:
         pl.semaphore_signal(far_sem, inc=1, device_id=peer, device_id_type=MESH)
 
-    a_copies = []
     for k in range(1, 16):
         to = plane_at[k - 1]
         copy = pltpu.make_async_remote_copy(
-            src_ref=a_send.at[to], dst_ref=a_recv.at[k - 1], send_sem=a_ssem.at[k - 1],
-            recv_sem=a_rsem.at[k - 1], device_id=plane_peers[k - 1], device_id_type=MESH,
-        )
-        copy.start()
-        a_copies.append(copy)
+            src_ref=a_send.at[to], dst_ref=a_recv.at[k - 1], send_sem=a_ssem,
+            recv_sem=a_rsem, device_id=plane_peers[k - 1], device_id_type=MESH,
+        )
+        copy.start()
 
     load_z.wait()
     empty = jnp.zeros((64, 64), F32)
@@ -191,18 +200,15 @@
 
     lax.fori_loop(0, 8, deposit_rows, 0)
 
-    d_copies = []
     for k in range(1, 16):
         to = plane_at[k - 1]
         copy = pltpu.make_async_remote_copy(
-            src_ref=d_send.at[to], dst_ref=d_recv.at[k - 1], send_sem=d_ssem.at[k - 1],
-            recv_sem=d_rsem.at[k - 1], device_id=plane_peers[k - 1], device_id_type=MESH,
-        )
-        copy.start()
-        d_copies.append(copy)
-
-    for copy in a_copies:
-        copy.wait_recv()
+            src_ref=d_send.at[to], dst_ref=d_recv.at[k - 1], send_sem=d_ssem,
+            recv_sem=d_rsem, device_id=plane_peers[k - 1], device_id_type=MESH,
+        )
+        copy.start()
+
+    a_stage.wait_recv()
     part = a_send[plane]
     for k in range(15):
         part = part + a_recv[k]
@@ -220,68 +226,60 @@
     ring_send[...] = (core_send[core] + core_recv[...]).astype(BF16)
 
     pl.semaphore_wait(far_sem, 2)
-    r_copies = []
     for k in range(1, 16):
         copy = pltpu.make_async_remote_copy(
             src_ref=ring_send.at[ring_at[k - 1] // 4], dst_ref=ring_recv.at[k - 1],
-            send_sem=r_ssem.at[k - 1], recv_sem=r_rsem.at[k - 1], device_id=ring_peers[k - 1],
+            send_sem=r_ssem, recv_sem=r_rsem, device_id=ring_peers[k - 1],
             device_id_type=MESH,
         )
         copy.start()
-        r_copies.append(copy)
-
-    for copy in d_copies:
-        copy.wait_recv()
+
+    d_stage.wait_recv()
     part = d_send[plane].astype(F32)
     for k in range(15):
         part = part + d_recv[k].astype(F32)
     e_send[...] = part.reshape(4, 8, 128)
-    e_copies = []
     for k in range(1, 4):
         copy = pltpu.make_async_remote_copy(
-            src_ref=e_send.at[low_at[k - 1]], dst_ref=e_recv.at[k - 1], send_sem=e_ssem.at[k - 1],
-            recv_sem=e_rsem.at[k - 1], device_id=low_peers[k - 1], device_id_type=MESH,
-        )
-        copy.start()
-        e_copies.append(copy)
-
-    for copy in r_copies:
-        copy.wait_recv()
+            src_ref=e_send.at[low_at[k - 1]], dst_ref=e_recv.at[k - 1], send_sem=e_ssem,
+            recv_sem=e_rsem, device_id=low_peers[k - 1], device_id_type=MESH,
+        )
+        copy.start()
+
+    r_stage.wait_recv()
     total = core_send[core, z_high_at] + core_recv[z_high_at]
     for k in range(15):
         total = total + ring_recv[k].astype(F32)
     slab_t[plane] = total.astype(BF16)
-    g_copies = []
     for k in range(1, 16):
         copy = pltpu.make_async_remote_copy(
-            src_ref=slab_t.at[plane], dst_ref=slab_t.at[plane], send_sem=g_ssem.at[k - 1],
-            recv_sem=g_rsem.at[k - 1], device_id=plane_peers[k - 1], device_id_type=MESH,
-        )
-        copy.start()
-        g_copies.append(copy)
+            src_ref=slab_t.at[plane], dst_ref=slab_t.at[plane], send_sem=g_ssem,
+            recv_sem=g_rsem, device_id=plane_peers[k - 1], device_id_type=MESH,
+        )
+        copy.start()
 
     own = jnp.where(z_low_at == 0, total[0:8], 0.0)
     for zc in range(1, 4):
         own = own + jnp.where(z_low_at == zc, total[8 * zc : 8 * (zc + 1)], 0.0)
     field_ref[0] = own[:, :64]
     field_ref[1] = own[:, 64:]
-    for copy in e_copies:
-        copy.wait_recv()
+    e_stage.wait_recv()
     own = e_send[z_low_at] + e_recv[0] + e_recv[1] + e_recv[2]
     deposit_ref[0] = own[:, :64]
     deposit_ref[1] = own[:, 64:]
     kicked_ref[...] = pushed[...]
 
-    for copy in g_copies:
-        copy.wait_recv()
+    for part in (a_stage, d_stage, e_stage, core_copy, r_stage):
+        part.wait_send()
+
+    g_stage.wait_recv()
     sampled = dot_tn(slab_t[...].reshape(512, 128), column_hot[...])
     longitudinal = jnp.sum(jnp.where(here, sampled[:64], 0.0), axis=0, keepdims=True)
     transverse = jnp.sum(jnp.where(here, sampled[64:], 0.0), axis=0, keepdims=True)
     kicked_ref[5:6, :] = pushed[5:6, :] + 0.5 * longitudinal
     kicked_ref[1:2, :] = pushed[1:2, :] + 0.5 * transverse
 
-    for copy in a_copies + d_copies + e_copies + [core_copy] + r_copies + g_copies:
-        copy.wait_send()
+    g_stage.wait_send()
 
 
 def place(kicked_in, field_in, deposit_in, kicked_ref, field_ref, deposit_ref, sems):
@@ -346,12 +344,12 @@
             pltpu.VMEM((128, 2048), BF16),
             pltpu.VMEM((6, 2048), F32),
             sem((12,)),
-            sem((15,)), sem((15,)),
-            sem((15,)), sem((15,)),
-            sem((3,)), sem((3,)),
             sem, sem,
-            sem((15,)), sem((15,)),
-            sem((15,)), sem((15,)), pltpu.SemaphoreType.REGULAR,
+            sem, sem,
+            sem, sem,
+            sem, sem,
+            sem, sem,
+            sem, sem, pltpu.SemaphoreType.REGULAR,
         ],
         compiler_params=pltpu.CompilerParams(
             collective_id=0, has_side_effects=True, vmem_limit_bytes=58 * 1024 * 1024

time: 38.6 us -> 37.4 us (0.969)
  Pallas kernels: 37.8 us -> 36.6 us
    pallas_call x1, Pallas kernels: 37.2 us -> 36 us  [local(): pl.pallas_call(kernel, out_shape=tuple((pltpu.VMEM(shape.shape, shape.dty...]
where the time goes in v3:
time: 37.4 us; the launch traced here: 37.3 us
  Pallas kernels  36.6 us (98%)
  between operations  0.64 us (2%)
    pallas_call x1, Pallas kernels, local(): pl.pallas_call(kernel, out_shape=tuple((pltpu.VMEM(shape.shape, shape.dty...  36 us

profile of v3, /device:TPU:1, one launch (start us, length us, event | category | flops | bytes accessed | tf_op | source)
XLA Modules:
  0.0 37.3 jit_solution(298852783648269461)
XLA Ops:
  0.6 36.0 %shard_map.139 = (f32[6,2048]{1,0:T(8,128)S(1)}, f32[2,8,64]{2,1,0:T(8,128)S(1)}, f32[2,8,64]{2,1,0:T(8,128)S(1)}) custom-call(f32[6,2048]{1,0:T(8,128)} %coords_hbm.1, f32[1,2048]{1,0:T(1,128)} %bitcast.7, s32[1,2048]{1,0:T(1,128)} %bitcast.8, s32[16]{0:T(128)} %block_hbm.1, s32[1,2048]{1,0:T(1,128)} %bitcast.9, f32[6,84]{1,0:T(8,128)} %map_hbm.1, ...), custom_call_target="tpu_custom_call" | custom-call | flops 1000000000 | bytes 4000000 | tf_op jit(solution)/shard_map/pallas_call | solution.py:309
  36.6 0.7 %shard_map.140 = (f32[6,2048]{1,0:T(8,128)}, f32[2,8,64]{2,1,0:T(8,128)}, f32[2,8,64]{2,1,0:T(8,128)}) custom-call(f32[6,2048]{1,0:T(8,128)S(1)} %get-tuple-element.9.kicked_in, f32[2,8,64]{2,1,0:T(8,128)S(1)} %get-tuple-element.10.field_in, f32[2,8,64]{2,1,0:T(8,128)S(1)} %get-tuple-element.11.deposit_in), custom_call_target="tpu_custom_call" | custom-call | bytes 100000 | tf_op jit(solution)/shard_map/pallas_call | solution.py:373

commit v4 on v3

--- a/solution.py
+++ b/solution.py
@@ -200,14 +200,6 @@
 
     lax.fori_loop(0, 8, deposit_rows, 0)
 
-    for k in range(1, 16):
-        to = plane_at[k - 1]
-        copy = pltpu.make_async_remote_copy(
-            src_ref=d_send.at[to], dst_ref=d_recv.at[k - 1], send_sem=d_ssem,
-            recv_sem=d_rsem, device_id=plane_peers[k - 1], device_id_type=MESH,
-        )
-        copy.start()
-
     a_stage.wait_recv()
     part = a_send[plane]
     for k in range(15):
@@ -234,6 +226,26 @@
         )
         copy.start()
 
+    for k in range(1, 16):
+        to = plane_at[k - 1]
+        copy = pltpu.make_async_remote_copy(
+            src_ref=d_send.at[to], dst_ref=d_recv.at[k - 1], send_sem=d_ssem,
+            recv_sem=d_rsem, device_id=plane_peers[k - 1], device_id_type=MESH,
+        )
+        copy.start()
+
+    r_stage.wait_recv()
+    total = core_send[core, z_high_at] + core_recv[z_high_at]
+    for k in range(15):
+        total = total + ring_recv[k].astype(F32)
+    slab_t[plane] = total.astype(BF16)
+    for k in range(1, 16):
+        copy = pltpu.make_async_remote_copy(
+            src_ref=slab_t.at[plane], dst_ref=slab_t.at[plane], send_sem=g_ssem,
+            recv_sem=g_rsem, device_id=plane_peers[k - 1], device_id_type=MESH,
+        )
+        copy.start()
+
     d_stage.wait_recv()
     part = d_send[plane].astype(F32)
     for k in range(15):
@@ -243,18 +255,6 @@
         copy = pltpu.make_async_remote_copy(
             src_ref=e_send.at[low_at[k - 1]], dst_ref=e_recv.at[k - 1], send_sem=e_ssem,
             recv_sem=e_rsem, device_id=low_peers[k - 1], device_id_type=MESH,
-        )
-        copy.start()
-
-    r_stage.wait_recv()
-    total = core_send[core, z_high_at] + core_recv[z_high_at]
-    for k in range(15):
-        total = total + ring_recv[k].astype(F32)
-    slab_t[plane] = total.astype(BF16)
-    for k in range(1, 16):
-        copy = pltpu.make_async_remote_copy(
-            src_ref=slab_t.at[plane], dst_ref=slab_t.at[plane], send_sem=g_ssem,
-            recv_sem=g_rsem, device_id=plane_peers[k - 1], device_id_type=MESH,
         )
         copy.start()
 

time: 37.4 us -> 37.1 us (level)
  no operation moved by 1% of the time
where the time goes in v4:
time: 37.1 us; the launch traced here: 36.9 us
  Pallas kernels  36.3 us (98%)
  between operations  0.64 us (2%)
    pallas_call x1, Pallas kernels, local(): pl.pallas_call(kernel, out_shape=tuple((pltpu.VMEM(shape.shape, shape.dty...  35.6 us

profile of v4, /device:TPU:1, one launch (start us, length us, event | category | flops | bytes accessed | tf_op | source)
XLA Modules:
  0.0 36.9 jit_solution(3344788148059983664)
XLA Ops:
  0.6 35.6 %shard_map.139 = (f32[6,2048]{1,0:T(8,128)S(1)}, f32[2,8,64]{2,1,0:T(8,128)S(1)}, f32[2,8,64]{2,1,0:T(8,128)S(1)}) custom-call(f32[6,2048]{1,0:T(8,128)} %coords_hbm.1, f32[1,2048]{1,0:T(1,128)} %bitcast.7, s32[1,2048]{1,0:T(1,128)} %bitcast.8, s32[16]{0:T(128)} %block_hbm.1, s32[1,2048]{1,0:T(1,128)} %bitcast.9, f32[6,84]{1,0:T(8,128)} %map_hbm.1, ...), custom_call_target="tpu_custom_call" | custom-call | flops 1000000000 | bytes 4000000 | tf_op jit(solution)/shard_map/pallas_call | solution.py:309
  36.3 0.7 %shard_map.140 = (f32[6,2048]{1,0:T(8,128)}, f32[2,8,64]{2,1,0:T(8,128)}, f32[2,8,64]{2,1,0:T(8,128)}) custom-call(f32[6,2048]{1,0:T(8,128)S(1)} %get-tuple-element.9.kicked_in, f32[2,8,64]{2,1,0:T(8,128)S(1)} %get-tuple-element.10.field_in, f32[2,8,64]{2,1,0:T(8,128)S(1)} %get-tuple-element.11.deposit_in), custom_call_target="tpu_custom_call" | custom-call | bytes 100000 | tf_op jit(solution)/shard_map/pallas_call | solution.py:373
